TPU v7x, 32 devices: a whole 2x2x4 slice. The times are simulated.
32 devices in a mesh: pre: 16 (over z, x, core), br: 2 (over y).
Axes of the slice: x: 2, y: 2, z: 4, core: 2. Of those that a mesh axis runs over, the one named last changes fastest.
Arguments:
- prompt_query: bfloat16 [1024, 8192], P('pre', 'br'), may hold values from -6 to 6
- prompt_key_rows: bfloat16 [1024, 1024], P('pre', 'br'), may hold values from -6 to 6
- prompt_value_rows: bfloat16 [1024, 1024], P('pre', 'br'), may hold values from -6 to 6
- prompt_grad_out: bfloat16 [1024, 8192], P('pre', 'br'), may hold values from -6 to 6
- prompt_lse: float32 [1024, 64], P('pre', 'br'), may hold values from 3 to 7
- prompt_delta: float32 [1024, 64], P('pre', 'br'), may hold values from -48 to 48
- resp_query: bfloat16 [2048, 8192], P(('pre', 'br')), may hold values from -6 to 6
- response_key_rows: bfloat16 [2048, 1024], P(('pre', 'br')), may hold values from -6 to 6
- response_value_rows: bfloat16 [2048, 1024], P(('pre', 'br')), may hold values from -6 to 6
- resp_grad_out: bfloat16 [2048, 8192], P(('pre', 'br')), may hold values from -6 to 6
- resp_lse: float32 [2048, 64], P(('pre', 'br')), may hold values from 3 to 7
- resp_delta: float32 [2048, 64], P(('pre', 'br')), may hold values from -48 to 48
- resp_segment: int32 [2048], P(('pre', 'br')), may hold values from -1 to 2047, as said below
Outputs:
- prompt_dq: bfloat16 [1024, 8192], P('pre', 'br')
- prompt_dk: bfloat16 [1024, 1024], P('pre', 'br')
- prompt_dv: bfloat16 [1024, 1024], P('pre', 'br')
- resp_dq: bfloat16 [2048, 8192], P(('pre', 'br'))
- response_key_gradient: bfloat16 [2048, 1024], P(('pre', 'br'))
- response_value_gradient: bfloat16 [2048, 1024], P(('pre', 'br'))
Inputs may be any that keep to these rules, and one draw needn't show every extreme that they name: `resp_segment`: each response occupies consecutive rows inside one aligned block of 64 rows and is named by the index of its first row; unused rows, which hold -1, stand at the end of a block; every block uses at least half of its rows, and block 0 holds one response of 64 rows.
All inputs are finite; a program needn't handle non-finite values.
Results may differ from a plain program's by a relative error of at most 0.007.
Values may be sent and summed in bfloat16 or wider, within the bound.
A program may use at most 128 MiB of HBM per device.

v0:
```python
import jax
import jax.numpy as jnp
from jax import lax
from jax.sharding import PartitionSpec as P

HEAD_SIZE = 128


def attend(query, grad_out, log_norm, row_term, keys, values, allowed):
    row_count = query.shape[0]
    key_count = keys.shape[0]
    groups = keys.shape[1] // HEAD_SIZE
    ratio = query.shape[1] // (groups * HEAD_SIZE)
    scaling = HEAD_SIZE ** (-0.5)
    query_heads = query.reshape(row_count, groups, ratio, HEAD_SIZE)
    grad_heads = grad_out.reshape(row_count, groups, ratio, HEAD_SIZE)
    key_heads = keys.reshape(key_count, groups, HEAD_SIZE)
    value_heads = values.reshape(key_count, groups, HEAD_SIZE)
    norm_t = log_norm.reshape(row_count, groups, ratio).transpose(1, 2, 0)[..., None]
    term_t = row_term.reshape(row_count, groups, ratio).transpose(1, 2, 0)[..., None]
    scores = (
        jnp.einsum("rgqd,ngd->gqrn", query_heads, key_heads, preferred_element_type=jnp.float32)
        * scaling
    )
    weights = jnp.where(allowed[None, None], jnp.exp(scores - norm_t), 0.0)
    dweights = jnp.einsum(
        "rgqd,ngd->gqrn", grad_heads, value_heads, preferred_element_type=jnp.float32
    )
    dscores = weights * (dweights - term_t)
    weights_b = weights.astype(jnp.bfloat16)
    dscores_b = dscores.astype(jnp.bfloat16)
    grad_v = jnp.einsum("gqrn,rgqd->ngd", weights_b, grad_heads, preferred_element_type=jnp.float32)
    grad_k = (
        jnp.einsum("gqrn,rgqd->ngd", dscores_b, query_heads, preferred_element_type=jnp.float32)
        * scaling
    )
    grad_q = (
        jnp.einsum("gqrn,ngd->rgqd", dscores_b, key_heads, preferred_element_type=jnp.float32)
        * scaling
    )
    return (
        grad_q.reshape(row_count, -1),
        grad_k.reshape(key_count, -1),
        grad_v.reshape(key_count, -1),
    )


def own_mask(segment):
    index = jnp.arange(segment.shape[0], dtype=jnp.int32)
    same = segment[:, None] == segment[None, :]
    return same & (segment[:, None] >= 0) & (index[None, :] <= index[:, None])


def add_rows(total, term, first_row):
    current = lax.dynamic_slice_in_dim(total, first_row, term.shape[0], 0)
    return lax.dynamic_update_slice_in_dim(total, current + term, first_row, 0)


def in_blocks(advance, totals, pieces, width):
    key_count = pieces[0].shape[0]
    stacked = tuple((piece.reshape(key_count // width, width, piece.shape[1]) for piece in pieces))
    offsets = jnp.arange(key_count // width, dtype=jnp.int32) * width

    def inner(running, entry):
        return (advance(running, entry[0], entry[1]), None)

    totals, unused = lax.scan(inner, totals, (stacked, offsets))
    return totals


def local(
    prompt_query,
    prompt_key_rows,
    prompt_value_rows,
    prompt_grad_out,
    prompt_lse,
    prompt_delta,
    resp_query,
    response_key_rows,
    response_value_rows,
    resp_grad_out,
    resp_lse,
    resp_delta,
    resp_segment,
):
    prompt_rows = prompt_query.shape[0]
    block_rows = resp_query.shape[0]
    prompt_total = prompt_rows * lax.axis_size("pre")
    prompt_pos = lax.axis_index("pre") * prompt_rows + jnp.arange(prompt_rows, dtype=jnp.int32)
    group_cols = prompt_key_rows.shape[1]
    moved_q, moved_go, moved_k, moved_v = (
        lax.all_to_all(resp_query, "br", split_axis=1, concat_axis=0, tiled=True),
        lax.all_to_all(resp_grad_out, "br", split_axis=1, concat_axis=0, tiled=True),
        lax.all_to_all(response_key_rows, "br", split_axis=1, concat_axis=0, tiled=True),
        lax.all_to_all(response_value_rows, "br", split_axis=1, concat_axis=0, tiled=True),
    )
    moved_norm, moved_term = (
        lax.all_to_all(resp_lse, "br", split_axis=1, concat_axis=0, tiled=True),
        lax.all_to_all(resp_delta, "br", split_axis=1, concat_axis=0, tiled=True),
    )
    moved_seg = lax.all_gather(resp_segment, "br", axis=0, tiled=True)
    resp_count = moved_q.shape[0]
    usable = moved_seg >= 0
    all_q = jnp.concatenate([prompt_query, moved_q], 0)
    all_go = jnp.concatenate([prompt_grad_out, moved_go], 0)
    all_norm = jnp.concatenate([prompt_lse, moved_norm], 0)
    all_term = jnp.concatenate([prompt_delta, moved_term], 0)
    blank_slot = jnp.zeros((prompt_total, group_cols), jnp.float32)
    start_totals = (jnp.zeros(all_q.shape, jnp.float32), blank_slot, blank_slot)

    def advance(totals, pieces, first_row):
        key_count = pieces[0].shape[0]
        key_pos = first_row + jnp.arange(key_count, dtype=jnp.int32)
        causal = key_pos[None, :] <= prompt_pos[:, None]
        allowed = jnp.concatenate(
            [causal, jnp.broadcast_to(usable[:, None], (resp_count, key_count))], 0
        )
        grad_q, grad_k, grad_v = attend(
            all_q, all_go, all_norm, all_term, pieces[0], pieces[1], allowed
        )
        return (
            totals[0] + grad_q,
            add_rows(totals[1], grad_k, first_row),
            add_rows(totals[2], grad_v, first_row),
        )

    dq_all, key_part, value_part = in_blocks(
        advance,
        start_totals,
        (
            lax.all_gather(prompt_key_rows, "pre", axis=0, tiled=True),
            lax.all_gather(prompt_value_rows, "pre", axis=0, tiled=True),
        ),
        prompt_rows,
    )
    prompt_dk, prompt_dv = (
        lax.psum_scatter(key_part, "pre", scatter_dimension=0, tiled=True),
        lax.psum_scatter(value_part, "pre", scatter_dimension=0, tiled=True),
    )
    block_total = resp_count // block_rows

    def self_terms(query, grad_out, log_norm, row_term, keys, values, segment):
        return attend(query, grad_out, log_norm, row_term, keys, values, own_mask(segment))

    near_q, near_k, near_v = jax.vmap(self_terms)(
        moved_q.reshape(block_total, block_rows, -1),
        moved_go.reshape(block_total, block_rows, -1),
        moved_norm.reshape(block_total, block_rows, -1),
        moved_term.reshape(block_total, block_rows, -1),
        moved_k.reshape(block_total, block_rows, -1),
        moved_v.reshape(block_total, block_rows, -1),
        moved_seg.reshape(block_total, block_rows),
    )
    head_dq = (dq_all[prompt_rows:] + near_q.reshape(resp_count, -1)).astype(jnp.bfloat16)
    head_dk = near_k.reshape(resp_count, -1).astype(jnp.bfloat16)
    head_dv = near_v.reshape(resp_count, -1).astype(jnp.bfloat16)
    resp_dq, response_key_gradient, response_value_gradient = (
        lax.all_to_all(head_dq, "br", split_axis=0, concat_axis=1, tiled=True),
        lax.all_to_all(head_dk, "br", split_axis=0, concat_axis=1, tiled=True),
        lax.all_to_all(head_dv, "br", split_axis=0, concat_axis=1, tiled=True),
    )
    prompt_dq = dq_all[:prompt_rows].astype(jnp.bfloat16)
    return (
        prompt_dq,
        prompt_dk.astype(jnp.bfloat16),
        prompt_dv.astype(jnp.bfloat16),
        resp_dq,
        response_key_gradient,
        response_value_gradient,
    )


def solution(mesh):
    in_specs = (
        P("pre", "br"),
        P("pre", "br"),
        P("pre", "br"),
        P("pre", "br"),
        P("pre", "br"),
        P("pre", "br"),
        P(("pre", "br"), None),
        P(("pre", "br"), None),
        P(("pre", "br"), None),
        P(("pre", "br"), None),
        P(("pre", "br"), None),
        P(("pre", "br"), None),
        P(("pre", "br")),
    )
    out_specs = (
        P("pre", "br"),
        P("pre", "br"),
        P("pre", "br"),
        P(("pre", "br"), None),
        P(("pre", "br"), None),
        P(("pre", "br"), None),
    )
    return jax.shard_map(local, mesh=mesh, in_specs=in_specs, out_specs=out_specs, check_vma=False)
```

profile of v0, /device:TPU:0, one launch (start us, length us, event | category | flops | bytes accessed | tf_op | source)
XLA Modules:
  0.0 721.0 jit_solution(8289373447688613948)
XLA Ops:
  10.2 4.2 all-to-all-start.1
  18.7 4.3 all-reduce
  23.0 3.3 all-to-all-start.3
  30.1 3.7 all-to-all-start
  36.2 10.1 %all-to-all-done = bf16[64,2,4096]{2,0,1:T(8,128)(2,1)S(1)} async-done(((bf16[64,2,4096]{2,0,1:T(8,128)(2,1)}), bf16[64,2,4096]{2,0,1:T(8,128)(2,1)S(1)}, u32[]{:S(2)}, u32[]{:S(2)}) %all-to-all-start) | async-done | bytes 1048608 | tf_op jit(solution)/shard_map/all_to_all | solution.py:92
  46.3 3.6 all-to-all-start.2
  51.3 10.2 %all-to-all-done.2 = bf16[64,2,4096]{2,0,1:T(8,128)(2,1)S(1)} async-done(((bf16[64,2,4096]{2,0,1:T(8,128)(2,1)}), bf16[64,2,4096]{2,0,1:T(8,128)(2,1)S(1)}, u32[]{:S(2)}, u32[]{:S(2)}) %all-to-all-start.2) | async-done | bytes 1048608 | tf_op jit(solution)/shard_map/all_to_all | solution.py:93
  62.9 27.0 %all-gather.5.cloned.1.call-done = bf16[1024,512]{1,0:T(8,128)(2,1)} async-done(((bf16[64,512]{1,0:T(8,128)(2,1)}), bf16[1024,512]{1,0:T(8,128)(2,1)}) %all-gather.5.cloned.1.call-update) | async-done | bytes 1048592 | tf_op jit(solution)/shard_map/all_gather | solution.py:132
  93.1 494.4 %while.15 = (s32[]{:T(128)}, f32[192,4096]{1,0:T(8,128)}, f32[1024,512]{1,0:T(8,128)}, f32[1024,512]{1,0:T(8,128)}, bf16[16,64,512]{2,1,0:T(8,128)(2,1)}, /*inde...) while((s32[]{:T(128)}, f32[192,4096]{1,0:T(8,128)}, ...), condition=%wide.region_1.2_spmd.clone, body=%wide.region_0.1_spmd.clone.sunk | while | flops 508543104 | bytes 59787072 | solution.py:67
  98.3 2.7 fusion.73
  108.2 2.5 fusion.75
  117.7 4.6 bitcast_add_fusion.5
  127.5 2.7 fusion.73
  137.4 2.5 fusion.75
  146.9 6.5 bitcast_add_fusion.5
  158.5 2.7 fusion.73
  168.4 2.5 fusion.75
  177.9 6.5 bitcast_add_fusion.5
  189.6 2.7 fusion.73
  199.5 2.5 fusion.75
  208.9 6.5 bitcast_add_fusion.5
  220.6 2.7 fusion.73
  239.9 6.5 bitcast_add_fusion.5
  251.6 2.7 fusion.73
  271.0 6.5 bitcast_add_fusion.5
  282.6 2.7 fusion.73
  302.0 6.5 bitcast_add_fusion.5
  313.7 2.7 fusion.73
  323.6 2.5 fusion.75
  333.0 6.5 bitcast_add_fusion.5
  344.7 2.7 fusion.73
  354.6 2.5 fusion.75
  364.0 6.5 bitcast_add_fusion.5
  375.7 2.7 fusion.73
  385.6 2.5 fusion.75
  395.1 6.5 bitcast_add_fusion.5
  406.7 2.7 fusion.73
  416.6 2.5 fusion.75
  426.1 6.5 bitcast_add_fusion.5
  437.8 2.7 fusion.73
  447.7 2.5 fusion.75
  457.1 6.5 bitcast_add_fusion.5
  468.8 2.7 fusion.73
  478.7 2.5 fusion.75
  488.1 6.5 bitcast_add_fusion.5
  499.8 2.7 fusion.73
  519.2 6.5 bitcast_add_fusion.5
  530.8 2.7 fusion.73
  550.2 6.5 bitcast_add_fusion.5
  561.9 2.7 fusion.73
  571.8 2.5 fusion.75
  581.1 6.5 bitcast_add_fusion.5
  589.1 3.4 all-to-all-start.4
  593.5 3.5 all-to-all-done.4
  597.0 3.6 all-to-all-start.5
  600.6 4.2 all-to-all-done.5
  609.9 3.4 all-to-all-start.7
  615.8 2.5 copy.83
  618.3 3.0 reshape.126
  622.0 3.4 all-to-all-start.8
  625.4 2.8 add_convert_fusion
  629.9 4.4 all-to-all-start.6
  636.5 9.0 %all-to-all-done.6 = bf16[2,64,4096]{2,1,0:T(8,128)(2,1)} async-done(((bf16[2,64,4096]{2,1,0:T(8,128)(2,1)}), bf16[2,64,4096]{2,1,0:T(8,128)(2,1)}, u32[]{:S(2)}, u32[]{:S(2)}) %all-to-all-start.6) | async-done | bytes 1048608 | tf_op jit(solution)/shard_map/all_to_all | solution.py:158
  649.7 63.2 %reduce-scatter.5.cloned.1.call-done = f32[64,512]{1,0:T(8,128)} async-done(((f32[1024,512]{1,0:T(8,128)}), f32[64,512]{1,0:T(8,128)}) %reduce-scatter.5.cloned.1.call-update) | async-done | bytes 131088 | tf_op jit(solution)/shard_map/reduce_scatter | solution.py:138
  (498 shorter events, 328.0 us)
Async XLA Ops:
  7.2 21.4 %copy-start.9 = (bf16[64,8192]{1,0:T(8,128)(2,1)S(1)}, bf16[64,8192]{1,0:T(8,128)(2,1)}, u32[]{:S(2)}) copy-start(bf16[64,8192]{1,0:T(8,128)(2,1)} %param.24) | copy-start | bytes 3145732
  7.2 55.7 %all-gather.3.cloned.1.call-start = ((), (), s32[]{:S(2)}) async-start(), calls=%async_computation.11 | async-start | bytes 1114112 | tf_op jit(solution)/shard_map/all_gather | solution.py:131
  7.9 82.0 %all-gather.5.cloned.1.call-start = ((), (), s32[]{:S(2)}) async-start(), calls=%async_computation.12 | async-start | bytes 1114112 | tf_op jit(solution)/shard_map/all_gather | solution.py:132
  10.2 12.8 %all-to-all-start.1 = ((f32[2,1,2048]{2,1,0:T(1,128)}), f32[2,1,2048]{2,1,0:T(1,128)S(1)}, u32[]{:S(2)}, u32[]{:S(2)}) async-start(f32[2,1,2048]{2,1,0:T(1,128)} %reshape.152), calls=%async_computation.1 | async-start | bytes 32768 | tf_op jit(solution)/shard_map/all_to_all | solution.py:98
  23.0 7.1 all-to-all-start.3
  30.1 19.8 %copy-start.14 = (f32[64,32]{0,1:T(8,128)S(1)}, f32[64,32]{0,1:T(8,128)}, u32[]{:S(2)}) copy-start(f32[64,32]{0,1:T(8,128)} %param.19) | copy-start | bytes 24580
  30.1 19.8 %copy-start.15 = (f32[64,32]{0,1:T(8,128)S(1)}, f32[64,32]{0,1:T(8,128)}, u32[]{:S(2)}) copy-start(f32[64,32]{0,1:T(8,128)} %param.20) | copy-start | bytes 24580
  30.1 19.9 %copy-start.10 = (bf16[64,4096]{1,0:T(8,128)(2,1)S(1)}, bf16[64,4096]{1,0:T(8,128)(2,1)}, u32[]{:S(2)}) copy-start(bf16[64,4096]{1,0:T(8,128)(2,1)} %param.15) | copy-start | bytes 1572868
  30.1 16.1 %all-to-all-start = ((bf16[64,2,4096]{2,0,1:T(8,128)(2,1)}), bf16[64,2,4096]{2,0,1:T(8,128)(2,1)S(1)}, u32[]{:S(2)}, u32[]{:S(2)}) async-start(bf16[64,2,4096]{2,0,1:T(8,128)(2,1)} %bitcast.173), calls=%async_computation | async-start | bytes 2097152 | tf_op jit(solution)/shard_map/all_to_all | solution.py:92
  46.3 5.0 copy-start.4
  46.3 15.2 %all-to-all-start.2 = ((bf16[64,2,4096]{2,0,1:T(8,128)(2,1)}), bf16[64,2,4096]{2,0,1:T(8,128)(2,1)S(1)}, u32[]{:S(2)}, u32[]{:S(2)}) async-start(bf16[64,2,4096]{2,0,1:T(8,128)(2,1)} %bitcast.172), calls=%async_computation.2 | async-start | bytes 2097152 | tf_op jit(solution)/shard_map/all_to_all | solution.py:93
  49.9 11.6 %copy-start.11 = (bf16[64,4096]{1,0:T(8,128)(2,1)S(1)}, bf16[64,4096]{1,0:T(8,128)(2,1)}, u32[]{:S(2)}) copy-start(bf16[64,4096]{1,0:T(8,128)(2,1)} %param.18) | copy-start | bytes 1572868
  49.9 598.3 %reduce-scatter.3.cloned.1.call-start = ((), (), s32[]{:S(2)}) async-start(), calls=%async_computation.13 | async-start | bytes 2228224 | tf_op jit(solution)/shard_map/reduce_scatter | solution.py:137
  61.5 30.1 %copy-start.6 = (bf16[64,2,4096]{2,0,1:T(8,128)(2,1)}, bf16[64,2,4096]{2,0,1:T(8,128)(2,1)S(1)}, u32[]{:S(2)}) copy-start(bf16[64,2,4096]{2,0,1:T(8,128)(2,1)S(1)} %all-to-all-done.2) | copy-start | bytes 3145732
  97.2 1.1 copy-start.2
  101.9 2.1 copy-start
  104.0 1.4 copy-start.3
  126.3 1.1 copy-start.2
  131.1 2.1 copy-start
  133.2 1.4 copy-start.3
  157.4 1.1 copy-start.2
  162.1 2.1 copy-start
  164.2 1.4 copy-start.3
  188.4 1.1 copy-start.2
  193.2 2.1 copy-start
  195.2 1.4 copy-start.3
  219.4 1.1 copy-start.2
  224.2 2.1 copy-start
  226.3 1.4 copy-start.3
  250.5 1.1 copy-start.2
  255.2 2.1 copy-start
  257.3 1.4 copy-start.3
  281.5 1.1 copy-start.2
  286.2 2.1 copy-start
  288.3 1.4 copy-start.3
  312.5 1.1 copy-start.2
  317.3 2.1 copy-start
  319.3 1.4 copy-start.3
  348.3 2.1 copy-start
  350.4 1.4 copy-start.3
  379.3 2.1 copy-start
  381.4 1.4 copy-start.3
  410.3 2.1 copy-start
  412.4 1.4 copy-start.3
  441.4 2.1 copy-start
  443.4 1.4 copy-start.3
  472.4 2.1 copy-start
  474.4 1.4 copy-start.3
  503.4 2.1 copy-start
  505.5 1.4 copy-start.3
  534.4 2.1 copy-start
  536.5 1.4 copy-start.3
  565.5 2.1 copy-start
  567.5 1.4 copy-start.3
  587.6 5.1 copy-start.13
  587.6 17.3 %copy-start.5 = (bf16[64,2,4096]{2,0,1:T(8,128)(2,1)S(1)}, bf16[64,2,4096]{2,0,1:T(8,128)(2,1)}, u32[]{:S(2)}) copy-start(bf16[64,2,4096]{2,0,1:T(8,128)(2,1)} %copy-done.4) | copy-start | bytes 3145732
  589.1 7.8 %all-to-all-start.4 = ((bf16[64,2,512]{2,0,1:T(8,128)(2,1)}), bf16[64,2,512]{2,0,1:T(8,128)(2,1)S(1)}, u32[]{:S(2)}, u32[]{:S(2)}) async-start(bf16[64,2,512]{2,0,1:T(8,128)(2,1)} %bitcast.177), calls=%async_computation.6 | async-start | bytes 262144 | tf_op jit(solution)/shard_map/all_to_all | solution.py:94
  592.5 120.4 %reduce-scatter.5.cloned.1.call-start = ((), (), s32[]{:S(2)}) async-start(), calls=%async_computation.14 | async-start | bytes 2228224 | tf_op jit(solution)/shard_map/reduce_scatter | solution.py:138
  593.4 11.7 %copy-start.7 = (bf16[64,2,4096]{2,0,1:T(8,128)(2,1)S(1)}, bf16[64,2,4096]{2,0,1:T(8,128)(2,1)}, u32[]{:S(2)}) copy-start(bf16[64,2,4096]{2,0,1:T(8,128)(2,1)} %copy-done.6) | copy-start | bytes 3145732
  597.0 7.8 %all-to-all-start.5 = ((bf16[64,2,512]{2,0,1:T(8,128)(2,1)}), bf16[64,2,512]{2,0,1:T(8,128)(2,1)S(1)}, u32[]{:S(2)}, u32[]{:S(2)}) async-start(bf16[64,2,512]{2,0,1:T(8,128)(2,1)} %bitcast.176), calls=%async_computation.7 | async-start | bytes 262144 | tf_op jit(solution)/shard_map/all_to_all | solution.py:95
  609.9 12.1 %all-to-all-start.7 = ((bf16[2,64,512]{2,1,0:T(8,128)(2,1)}), bf16[2,64,512]{2,1,0:T(8,128)(2,1)S(1)}, u32[]{:S(2)}, u32[]{:S(2)}) async-start(bf16[2,64,512]{2,1,0:T(8,128)(2,1)} %bitcast.175), calls=%async_computation.9 | async-start | bytes 262144 | tf_op jit(solution)/shard_map/all_to_all | solution.py:159
  618.3 7.1 copy-start.1
  622.0 7.9 %all-to-all-start.8 = ((bf16[2,64,512]{2,1,0:T(8,128)(2,1)}), bf16[2,64,512]{2,1,0:T(8,128)(2,1)S(1)}, u32[]{:S(2)}, u32[]{:S(2)}) async-start(bf16[2,64,512]{2,1,0:T(8,128)(2,1)} %bitcast.174), calls=%async_computation.10 | async-start | bytes 262144 | tf_op jit(solution)/shard_map/all_to_all | solution.py:160
  629.9 15.6 %all-to-all-start.6 = ((bf16[2,64,4096]{2,1,0:T(8,128)(2,1)}), bf16[2,64,4096]{2,1,0:T(8,128)(2,1)}, u32[]{:S(2)}, u32[]{:S(2)}) async-start(bf16[2,64,4096]{2,1,0:T(8,128)(2,1)} %bitcast.232), calls=%async_computation.8 | async-start | bytes 2097152 | tf_op jit(solution)/shard_map/all_to_all | solution.py:158
  (10 other events, 11.1 us)
Sparse Core Ops, SparseCore 0:
  10.2 40.6 all-gather.2
  53.0 36.8 all-gather.4
  587.7 60.4 reduce-scatter.2
  652.3 60.6 reduce-scatter.4
where the time goes:
time: 727 us; the launch traced here: 721 us
  local copies, waits for them, and re-layouts  232 us (32%)
  other arithmetic  140 us (19%)
  matrix products  133 us (18%)
  waiting for transfers between devices  131 us (18%)
  starting transfers between devices  33.1 us (5%)
  loops' own time  32.7 us (4%)
  between operations  14.7 us (2%)
    add x16, other arithmetic, advance(): totals[0] + grad_q  102 us
    while x128, local copies, waits for them, and re-layouts  83 us
    reduce_scatter x1, waiting for transfers between devices, local(): lax.psum_scatter(value_part, 'pre', scatter_dimension=0, tiled=True)  63.2 us
    dynamic_update_slice x32, local copies, waits for them, and re-layouts, add_rows(): return lax.dynamic_update_slice_in_dim(total, current + term, first_row, 0)  53.4 us
    dot_general x17, matrix products, attend(): jnp.einsum('rgqd,ngd->gqrn', query_heads, key_heads, preferred_element_ty...  44.8 us
    dot_general x17, matrix products, attend(): jnp.einsum('gqrn,rgqd->ngd', weights_b, grad_heads, preferred_element_typ...  40.9 us
    dynamic_slice x48, local copies, waits for them, and re-layouts, in_blocks(): totals, unused = lax.scan(inner, totals, (stacked, offsets))  36.4 us
    another operation x1, loops' own time, in_blocks(): totals, unused = lax.scan(inner, totals, (stacked, offsets))  32.7 us
  transfers between devices with their start and end apart: 13, of which 10 were waited for; matrix products, arithmetic and copies ran while one was open for 5% of the time, Pallas kernels for 0%

commit v1 on v0

v1 whole, which is shorter than its diff:
```python
import functools

import jax
import jax.numpy as jnp
from jax import lax
from jax.experimental import pallas as pl
from jax.experimental.pallas import tpu as pltpu
from jax.sharding import PartitionSpec as P

HEAD = 128
SCALE = HEAD ** (-0.5)
LOG2E = 1.4426950408889634
F32 = jnp.float32
BF16 = jnp.bfloat16


def dot(a, b, ca, cb):
    return lax.dot_general(a, b, (((ca,), (cb,)), ((), ())), preferred_element_type=F32)


def stack_heads(block):
    ratio = block.shape[1] // HEAD
    return jnp.concatenate([block[:, h * HEAD : (h + 1) * HEAD] for h in range(ratio)], 0)


def spread_heads(dq_t, rows):
    dq = dq_t.T
    ratio = dq.shape[0] // rows
    return jnp.concatenate([dq[h * rows : (h + 1) * rows] for h in range(ratio)], 1)


def terms(k, v, q, go, norm, delta, bias):
    s = dot(k, q, 1, 1)
    z = s * (SCALE * LOG2E) - norm
    if bias is not None:
        z = z + bias
    w = jnp.exp2(z)
    ds = w * (dot(v, go, 1, 1) - delta)
    wb = w.astype(BF16)
    dsb = ds.astype(BF16)
    return dot(dsb, q, 1, 0) * SCALE, dot(wb, go, 1, 0), dot(k, dsb, 0, 0)


def attention_kernel(
    chunk_blocks,
    place,
    kv_ref,
    rq_ref,
    rgo_ref,
    rnorm_ref,
    rdelta_ref,
    bias_ref,
    rk_ref,
    rv_ref,
    pq_ref,
    pgo_ref,
    pnorm_ref,
    pdelta_ref,
    dkv_ref,
    rdq_ref,
    rdk_ref,
    rdv_ref,
    pdq_ref,
    racc,
    pacc,
):
    n_pre, _, _, block_rows, _ = kv_ref.shape
    group = pl.program_id(0)
    pre = place[0]
    per_br = place[2]
    mine = (group // per_br) == place[1]
    rows = rq_ref.shape[0]
    prow = pq_ref.shape[0]
    chunk = chunk_blocks * block_rows
    rq = stack_heads(rq_ref[...])
    rgo = stack_heads(rgo_ref[...])
    rnorm = rnorm_ref[0]
    rdelta = rdelta_ref[0]
    dk, dv, dq = terms(rk_ref[...], rv_ref[...], rq, rgo, rnorm, rdelta, bias_ref[...])
    rdk_ref[...] = dk.astype(BF16)
    rdv_ref[...] = dv.astype(BF16)
    racc[...] = dq

    @pl.when(mine)
    def _():
        pacc[...] = jnp.zeros_like(pacc)

    for c in range(n_pre // chunk_blocks):
        at = pl.ds(c * chunk_blocks, chunk_blocks)
        k = kv_ref[at, 0, 0].reshape(chunk, HEAD)
        v = kv_ref[at, 0, 1].reshape(chunk, HEAD)
        dk, dv, dq = terms(k, v, rq, rgo, rnorm, rdelta, None)
        racc[...] += dq
        with_prompt = mine & (c * chunk < (pre + 1) * prow)

        @pl.when(with_prompt)
        def _():
            pq = stack_heads(pq_ref[...])
            pgo = stack_heads(pgo_ref[...])
            key = lax.broadcasted_iota(jnp.int32, (chunk, pq.shape[0]), 0) + c * chunk
            row = lax.rem(lax.broadcasted_iota(jnp.int32, (chunk, pq.shape[0]), 1), prow)
            bias = jnp.where(key <= row + pre * prow, 0.0, -1e30)
            pdk, pdv, pdq = terms(k, v, pq, pgo, pnorm_ref[0], pdelta_ref[0], bias)
            pacc[...] += pdq
            dkv_ref[at, 0, 0] = (dk + pdk).reshape(chunk_blocks, block_rows, HEAD)
            dkv_ref[at, 0, 1] = (dv + pdv).reshape(chunk_blocks, block_rows, HEAD)

        @pl.when(jnp.logical_not(with_prompt))
        def _():
            dkv_ref[at, 0, 0] = dk.reshape(chunk_blocks, block_rows, HEAD)
            dkv_ref[at, 0, 1] = dv.reshape(chunk_blocks, block_rows, HEAD)

    rdq_ref[...] = (spread_heads(racc[...], rows) * SCALE).astype(BF16)

    @pl.when(mine)
    def _():
        pdq_ref[...] = (spread_heads(pacc[...], prow) * SCALE).astype(BF16)


def per_group(x, groups):
    rows, heads = x.shape
    return x.T.reshape(groups, 1, heads // groups * rows)


def local(
    n_pre,
    n_br,
    prompt_query,
    prompt_key_rows,
    prompt_value_rows,
    prompt_grad_out,
    prompt_lse,
    prompt_delta,
    resp_query,
    response_key_rows,
    response_value_rows,
    resp_grad_out,
    resp_lse,
    resp_delta,
    resp_segment,
):
    prow, cols = prompt_key_rows.shape
    rows, width = response_key_rows.shape
    groups = width // HEAD
    per_br = cols // HEAD
    ratio = resp_query.shape[1] // width
    wide = ratio * HEAD
    pre = lax.axis_index("pre").astype(jnp.int32)
    br = lax.axis_index("br").astype(jnp.int32)
    place = jnp.stack([pre, br, jnp.int32(per_br)])

    kv = jnp.stack([prompt_key_rows, prompt_value_rows])
    kv_all = lax.all_gather(kv, ("pre", "br"), axis=0, tiled=False)
    kv_all = kv_all.reshape(n_pre, n_br, 2, prow, cols)

    usable = (resp_segment >= 0)[:, None]
    rnorm = per_group(jnp.where(usable, resp_lse * LOG2E, 1e30), groups)
    rdelta = per_group(resp_delta, groups)
    pnorm = per_group(prompt_lse * LOG2E, per_br)
    pdelta = per_group(prompt_delta, per_br)
    index = jnp.arange(rows, dtype=jnp.int32)
    seen = (resp_segment[:, None] == resp_segment[None, :]) & (index[:, None] <= index[None, :])
    bias = jnp.tile(jnp.where(seen, 0.0, -1e30), (1, ratio))

    def kv_at(g, place):
        return (0, g // per_br, 0, 0, g % per_br)

    def prompt_g(g, place):
        return jnp.clip(g - place[1] * per_br, 0, per_br - 1)

    chunk_blocks = max(1, 256 // prow)
    col = lambda g, place: (0, g)
    pcol = lambda g, place: (0, prompt_g(g, place))
    lead = lambda g, place: (g, 0, 0)
    plead = lambda g, place: (prompt_g(g, place), 0, 0)
    dkv, rdq, rdk, rdv, pdq = pl.pallas_call(
        functools.partial(attention_kernel, chunk_blocks),
        grid_spec=pltpu.PrefetchScalarGridSpec(
            num_scalar_prefetch=1,
            grid=(groups,),
            in_specs=[
                pl.BlockSpec((n_pre, 1, 2, prow, HEAD), kv_at),
                pl.BlockSpec((rows, wide), col),
                pl.BlockSpec((rows, wide), col),
                pl.BlockSpec((1, 1, ratio * rows), lead),
                pl.BlockSpec((1, 1, ratio * rows), lead),
                pl.BlockSpec((rows, ratio * rows), lambda g, place: (0, 0)),
                pl.BlockSpec((rows, HEAD), col),
                pl.BlockSpec((rows, HEAD), col),
                pl.BlockSpec((prow, wide), pcol),
                pl.BlockSpec((prow, wide), pcol),
                pl.BlockSpec((1, 1, ratio * prow), plead),
                pl.BlockSpec((1, 1, ratio * prow), plead),
            ],
            out_specs=[
                pl.BlockSpec((n_pre, 1, 2, prow, HEAD), kv_at),
                pl.BlockSpec((rows, wide), col),
                pl.BlockSpec((rows, HEAD), col),
                pl.BlockSpec((rows, HEAD), col),
                pl.BlockSpec((prow, wide), pcol),
            ],
            scratch_shapes=[
                pltpu.VMEM((HEAD, ratio * rows), F32),
                pltpu.VMEM((HEAD, ratio * prow), F32),
            ],
        ),
        out_shape=[
            jax.ShapeDtypeStruct((n_pre, n_br, 2, prow, cols), F32),
            jax.ShapeDtypeStruct(resp_query.shape, BF16),
            jax.ShapeDtypeStruct(response_key_rows.shape, BF16),
            jax.ShapeDtypeStruct(response_value_rows.shape, BF16),
            jax.ShapeDtypeStruct(prompt_query.shape, BF16),
        ],
        compiler_params=pltpu.CompilerParams(vmem_limit_bytes=48 * 1024 * 1024),
        name="attention",
    )(
        place,
        kv_all,
        resp_query,
        resp_grad_out,
        rnorm,
        rdelta,
        bias,
        response_key_rows,
        response_value_rows,
        prompt_query,
        prompt_grad_out,
        pnorm,
        pdelta,
    )
    total = lax.psum_scatter(
        dkv.reshape(n_pre * n_br, 2, prow, cols), ("pre", "br"), scatter_dimension=0, tiled=False
    )
    return pdq, total[0].astype(BF16), total[1].astype(BF16), rdq, rdk, rdv


def solution(mesh):
    both = P("pre", "br")
    own = P(("pre", "br"), None)
    in_specs = (both,) * 6 + (own,) * 6 + (P(("pre", "br")),)
    out_specs = (both,) * 3 + (own,) * 3
    body = functools.partial(local, mesh.shape["pre"], mesh.shape["br"])
    return jax.shard_map(body, mesh=mesh, in_specs=in_specs, out_specs=out_specs, check_vma=False)
```

time: 727 us -> 308 us (0.42)
  local copies, waits for them, and re-layouts: 232 us -> 9.11 us
  other arithmetic: 140 us -> 5.6 us
  matrix products: 133 us -> 0 us
  waiting for transfers between devices: 131 us -> 250 us
  starting transfers between devices: 33.1 us -> 0.08 us
  loops' own time: 32.7 us -> 0 us
  Pallas kernels: 0 us -> 28.5 us
    dot_general x85 -> x0, matrix products: 133 us -> none  [the longest x17 44.8 us: attend(): jnp.einsum('rgqd,ngd->gqrn', query_heads, key_heads, preferred_element_ty...]
    add x64 -> x0, other arithmetic: 129 us -> none  [the longest x16 102 us: advance(): totals[0] + grad_q]
    reduce_scatter x2 -> x1, waiting for transfers between devices: 63.7 us -> 188 us  [local(): lax.psum_scatter(dkv.reshape(n_pre * n_br, 2, prow, cols), ('pre', 'br'),...]
    while x128 -> x0, local copies, waits for them, and re-layouts: 83 us -> none
    dynamic_update_slice x32 -> x0, local copies, waits for them, and re-layouts: 53.4 us -> none  [add_rows(): return lax.dynamic_update_slice_in_dim(total, current + term, first_row, 0)]
    all_to_all x9 -> x0, waiting for transfers between devices: 39.1 us -> none  [the longest x1 10.2 us: local(): lax.all_to_all(resp_grad_out, 'br', split_axis=1, concat_axis=0, tiled=True)]
    dynamic_slice x48 -> x0, local copies, waits for them, and re-layouts: 36.4 us -> none  [in_blocks(): totals, unused = lax.scan(inner, totals, (stacked, offsets))]
    all_gather x2 -> x1, waiting for transfers between devices: 27 us -> 62.2 us  [local(): kv_all = lax.all_gather(kv, ('pre', 'br'), axis=0, tiled=False)]
  transfers between devices with their start and end apart: 13 -> 2, of which waited for: 10 -> 2; matrix products, arithmetic and copies ran while one was open for 5% -> 2% of each run, Pallas kernels for 0% -> 0%
where the time goes in v1:
time: 308 us
  waiting for transfers between devices  250 us (81%)
  Pallas kernels  28.5 us (9%)
  between operations  14.1 us (5%)
  local copies, waits for them, and re-layouts  9.11 us (3%)
  other arithmetic  5.6 us (2%)
    reduce_scatter x1, waiting for transfers between devices, local(): lax.psum_scatter(dkv.reshape(n_pre * n_br, 2, prow, cols), ('pre', 'br'),...  188 us
    all_gather x1, waiting for transfers between devices, local(): kv_all = lax.all_gather(kv, ('pre', 'br'), axis=0, tiled=False)  62.2 us
    pallas_call x1, Pallas kernels, local(): pl.pallas_call(functools.partial(attention_kernel, chunk_blocks), grid_sp...  28.5 us
    unnamed x12, local copies, waits for them, and re-layouts  6.34 us
  transfers between devices with their start and end apart: 2, of which 2 were waited for; matrix products, arithmetic and copies ran while one was open for 2% of the time, Pallas kernels for 0%

profile of v1, /device:TPU:0, one launch (start us, length us, event | category | flops | bytes accessed | tf_op | source)
XLA Modules:
  0.0 307.8 jit_solution(5794987317660054407)
XLA Ops:
  7.2 0.0 all-gather.3.cloned.1.call-start
  7.2 1.5 pad_maximum_fusion
  8.8 0.0 all-gather.3.cloned.1.call-update
  8.8 0.0 reduce-scatter.2.cloned.1.call-start
  8.8 0.8 reshape.84.pdelta_ref
  9.6 0.7 multiply_bitcast_fusion
  10.4 0.1 reshape.83.pnorm_ref
  10.4 0.7 broadcast_compare_fusion
  11.1 0.8 select_bitcast_fusion
  11.9 0.1 copy.21
  12.0 0.1 reshape.81.rnorm_ref
  12.1 0.8 copy.22
  12.9 0.1 reshape.82.rdelta_ref
  13.0 0.8 fusion.1
  13.9 0.1 tile.10.bias_ref
  14.0 0.1 pad_add_fusion.place
  14.1 62.2 %all-gather.3.cloned.1.call-done = bf16[64,64,512]{2,1,0:T(8,128)(2,1)} async-done(((bf16[2,64,512]{2,1,0:T(8,128)(2,1)}), bf16[64,64,512]{2,1,0:T(8,128)(2,1)}) %all-gather.3.cloned.1.call-update) | async-done | bytes 4194320 | tf_op jit(solution)/shard_map/all_gather | solution.py:153
  76.3 0.0 copy-start
  76.3 1.2 copy-done
  77.5 0.0 copy-start.1
  77.5 1.2 copy-done.1
  78.7 0.0 copy-start.2
  78.7 1.0 copy-done.2
  79.8 0.0 copy-start.3
  79.8 1.0 copy-done.3
  80.8 0.0 copy-start.4
  80.8 0.9 copy-done.4
  81.7 0.0 copy-start.5
  81.7 0.9 copy-done.5
  82.6 28.5 %attention.1 = (f32[16,2,2,64,512]{4,3,2,1,0:T(8,128)}, bf16[64,8192]{1,0:T(8,128)(2,1)}, bf16[64,1024]{1,0:T(8,128)(2,1)}, bf16[64,1024]{1,0:T(8,128)(2,1)}, bf16[64,4096]{1,0:T(8,128)(2,1)}) custom-call(s32[3]{0:T(128)S(1)} %pad_add_fusion.place, bf16[16,2,2,64,512]{4,3,2,1,0:T(8,128)(2,1)} %bitcast.17, bf16[64,8192]{1,0:T(8,128)(2,1)S(1)} %copy-done, ...), custom_call_target="tpu_custom_call" | custom-call | tf_op jit(solution)/shard_map/attention/pallas_call | solution.py:176
  111.1 0.0 reduce-scatter.2.cloned.1.call-update
  111.1 188.2 %reduce-scatter.2.cloned.1.call-done = f32[1,2,64,512]{3,2,1,0:T(8,128)} async-done(((f32[32,2,64,512]{3,2,1,0:T(8,128)}), f32[1,2,64,512]{3,2,1,0:T(8,128)}) %reduce-scatter.2.cloned.1.call-update) | async-done | bytes 262160 | tf_op jit(solution)/shard_map/reduce_scatter | solution.py:231
  299.3 1.0 convert.4
  300.3 0.7 slice_bitcast_fusion
  (1 shorter events, 0.0 us)
Async XLA Ops:
  7.2 69.1 %all-gather.3.cloned.1.call-start = ((), (), s32[]{:S(2)}) async-start(), calls=%async_computation.2 | async-start | bytes 4325376 | tf_op jit(solution)/shard_map/all_gather | solution.py:153
  8.8 290.5 %reduce-scatter.2.cloned.1.call-start = ((), (), s32[]{:S(2)}) async-start(), calls=%async_computation.1 | async-start | bytes 8650752 | tf_op jit(solution)/shard_map/reduce_scatter | solution.py:231
  76.3 1.2 copy-start
  77.5 1.2 copy-start.1
  78.7 1.0 copy-start.2
  79.8 1.0 copy-start.3
  80.8 0.9 copy-start.4
  81.7 0.9 copy-start.5
Sparse Core Ops, SparseCore 0:
  11.5 64.7 all-gather.2
  111.2 188.0 reduce-scatter.1

commit v2 on v1

--- a/solution.py
+++ b/solution.py
@@ -102,19 +102,248 @@
             bias = jnp.where(key <= row + pre * prow, 0.0, -1e30)
             pdk, pdv, pdq = terms(k, v, pq, pgo, pnorm_ref[0], pdelta_ref[0], bias)
             pacc[...] += pdq
-            dkv_ref[at, 0, 0] = (dk + pdk).reshape(chunk_blocks, block_rows, HEAD)
-            dkv_ref[at, 0, 1] = (dv + pdv).reshape(chunk_blocks, block_rows, HEAD)
+            dkv_ref[at, 0, 0] = (dk + pdk).astype(BF16).reshape(chunk_blocks, block_rows, HEAD)
+            dkv_ref[at, 0, 1] = (dv + pdv).astype(BF16).reshape(chunk_blocks, block_rows, HEAD)
 
         @pl.when(jnp.logical_not(with_prompt))
         def _():
-            dkv_ref[at, 0, 0] = dk.reshape(chunk_blocks, block_rows, HEAD)
-            dkv_ref[at, 0, 1] = dv.reshape(chunk_blocks, block_rows, HEAD)
+            dkv_ref[at, 0, 0] = dk.astype(BF16).reshape(chunk_blocks, block_rows, HEAD)
+            dkv_ref[at, 0, 1] = dv.astype(BF16).reshape(chunk_blocks, block_rows, HEAD)
 
     rdq_ref[...] = (spread_heads(racc[...], rows) * SCALE).astype(BF16)
 
     @pl.when(mine)
     def _():
         pdq_ref[...] = (spread_heads(pacc[...], prow) * SCALE).astype(BF16)
+
+
+def position(nz, ny):
+    pre = lax.axis_index("pre")
+    y = lax.axis_index("br")
+    z = pre // 4
+    x = lax.rem(pre // 2, 2)
+    c = lax.rem(pre, 2)
+    index = lambda zz, xx, cc: (zz * 2 + xx) * 2 + cc
+    around_z = [lax.rem(z + d, nz) for d in range(1, nz)]
+    around_y = [lax.rem(y + d, ny) for d in range(1, ny)]
+    return z, x, c, y, index, around_z, around_y
+
+
+def greet(targets):
+    barrier = pltpu.get_barrier_semaphore()
+    for target in targets:
+        pl.semaphore_signal(barrier, inc=1, device_id=target, device_id_type=pl.DeviceIdType.MESH)
+    pl.semaphore_wait(barrier, len(targets))
+
+
+def gather_kernel(nz, ny, own_ref, out_ref, send_sem, recv_sem, local_sem):
+    z, x, c, y, index, around_z, around_y = position(nz, ny)
+    sibling = (index(z, x, 1 - c), y)
+    x_side = (index(z, 1 - x, c), y)
+    y_side = [(index(z, x, c), yy) for yy in around_y]
+    z_side = [(index(zz, x, c), y) for zz in around_z]
+    greet([sibling, x_side] + y_side + z_side)
+    sent = []
+
+    def send(zz, xx, yy, t, target, mine=False):
+        slot = index(zz, xx, c)
+        copy = pltpu.make_async_remote_copy(
+            src_ref=own_ref.at[t] if mine else out_ref.at[slot, yy, t],
+            dst_ref=out_ref.at[slot, yy, t],
+            send_sem=send_sem.at[len(sent)],
+            recv_sem=recv_sem.at[slot, yy, t],
+            device_id=target,
+            device_id_type=pl.DeviceIdType.MESH,
+        )
+        copy.start()
+        sent.append(copy)
+
+    def arrive(zz, xx, yy, cc, t):
+        at = out_ref.at[index(zz, xx, cc), yy, t]
+        pltpu.make_async_copy(at, at, recv_sem.at[index(zz, xx, cc), yy, t]).wait()
+
+    def column(zz, mine):
+        for t in range(2):
+            if not mine:
+                arrive(zz, x, y, c, t)
+            send(zz, x, y, t, x_side, mine)
+            for target in y_side:
+                send(zz, x, y, t, target, mine)
+            send(zz, x, y, t, sibling, mine)
+
+    def second(zz):
+        for t in range(2):
+            arrive(zz, 1 - x, y, c, t)
+            if t == 0:
+                for target in y_side:
+                    send(zz, 1 - x, y, 0, target)
+            send(zz, 1 - x, y, t, sibling)
+            for yy in around_y:
+                arrive(zz, x, yy, c, t)
+                if t == 1:
+                    send(zz, x, yy, 1, x_side)
+                send(zz, x, yy, t, sibling)
+
+    def third(zz):
+        for t in range(2):
+            for yy in around_y:
+                arrive(zz, 1 - x, yy, c, t)
+                send(zz, 1 - x, yy, t, sibling)
+
+    for target in z_side:
+        for t in range(2):
+            send(z, x, y, t, target, True)
+    keep = pltpu.make_async_copy(own_ref, out_ref.at[index(z, x, c), y], local_sem)
+    keep.start()
+    order = [z] + around_z
+    for step in range(nz + 2):
+        if step < nz:
+            column(order[step], step == 0)
+        if 0 <= step - 1 < nz:
+            second(order[step - 1])
+        if 0 <= step - 2 < nz:
+            third(order[step - 2])
+    for zz in order:
+        for xx in range(2):
+            for yy in [y] + around_y:
+                for t in range(2):
+                    arrive(zz, xx, yy, 1 - c, t)
+    keep.wait()
+    for copy in sent:
+        copy.wait_send()
+
+
+def gather(own, n_pre, n_br):
+    nz = n_pre // 4
+    copies = 2 * (nz - 1) + nz * (2 * (1 + n_br) + (n_br - 1) * 2 + 2 * n_br + 2 * (n_br - 1))
+    return pl.pallas_call(
+        functools.partial(gather_kernel, nz, n_br),
+        out_shape=jax.ShapeDtypeStruct((n_pre, n_br) + own.shape, BF16),
+        in_specs=[pl.BlockSpec(memory_space=pl.ANY)],
+        out_specs=pl.BlockSpec(memory_space=pl.ANY),
+        scratch_shapes=[
+            pltpu.SemaphoreType.DMA((copies,)),
+            pltpu.SemaphoreType.DMA((n_pre, n_br, 2)),
+            pltpu.SemaphoreType.DMA,
+        ],
+        compiler_params=pltpu.CompilerParams(collective_id=0, has_side_effects=True),
+        name="gather_keys",
+    )(own)
+
+
+def reduce_kernel(
+    nz, ny, part_ref, out_ref, r0, rx, ry, ryk, rxv, sz, rz, send_sem, q0, qx, qy, qyk, qxv, qz
+):
+    z, x, c, y, index, around_z, around_y = position(nz, ny)
+    sibling = (index(z, x, 1 - c), y)
+    x_side = (index(z, 1 - x, c), y)
+    y_side = [(index(z, x, c), yy) for yy in around_y]
+    z_side = [(index(zz, x, c), y) for zz in around_z]
+    greet([sibling, x_side] + y_side + z_side)
+    order = around_z + [z]
+    sent = []
+
+    def send(src, dst, sem, target):
+        copy = pltpu.make_async_remote_copy(
+            src_ref=src,
+            dst_ref=dst,
+            send_sem=send_sem.at[len(sent)],
+            recv_sem=sem,
+            device_id=target,
+            device_id_type=pl.DeviceIdType.MESH,
+        )
+        copy.start()
+        sent.append(copy)
+
+    def arrive(at, sem):
+        pltpu.make_async_copy(at, at, sem).wait()
+
+    for i, zz in enumerate(order):
+        send(part_ref.at[zz, :, 1 - c], r0.at[i], q0.at[i], sibling)
+
+    def first(i):
+        arrive(r0.at[i], q0.at[i])
+        for xx in range(2):
+            for yy in range(ny):
+                own = part_ref[order[i], xx, c, yy].astype(F32)
+                r0[i, xx, yy] = (own + r0[i, xx, yy].astype(F32)).astype(BF16)
+        send(r0.at[i, 1 - x, :, 0], rx.at[i], qx.at[i], x_side)
+        for target, yy in zip(y_side, around_y):
+            send(r0.at[i, :, yy, 1], ry.at[i, y], qy.at[i, y], target)
+
+    def second(i):
+        arrive(rx.at[i], qx.at[i])
+        rx[i] = (r0[i, x, :, 0].astype(F32) + rx[i].astype(F32)).astype(BF16)
+        for target, yy in zip(y_side, around_y):
+            send(rx.at[i, yy], ryk.at[i, y], qyk.at[i, y], target)
+        total = r0[i, :, y, 1].astype(F32)
+        for yy in around_y:
+            arrive(ry.at[i, yy], qy.at[i, yy])
+            total = total + ry[i, yy].astype(F32)
+        ry[i, y] = total.astype(BF16)
+        send(ry.at[i, y, 1 - x], rxv.at[i], qxv.at[i], x_side)
+
+    def third(i):
+        total_k = rx[i, y].astype(F32)
+        for yy in around_y:
+            arrive(ryk.at[i, yy], qyk.at[i, yy])
+            total_k = total_k + ryk[i, yy].astype(F32)
+        arrive(rxv.at[i], qxv.at[i])
+        total_v = ry[i, y, x].astype(F32) + rxv[i].astype(F32)
+        if i < nz - 1:
+            sz[i, 0] = total_k.astype(BF16)
+            sz[i, 1] = total_v.astype(BF16)
+            send(sz.at[i], rz.at[i], qz.at[i], z_side[i])
+            return
+        for j in range(nz - 1):
+            arrive(rz.at[j], qz.at[j])
+            total_k = total_k + rz[j, 0].astype(F32)
+            total_v = total_v + rz[j, 1].astype(F32)
+        out_ref[0] = total_k.astype(BF16)
+        out_ref[1] = total_v.astype(BF16)
+
+    for step in range(nz + 2):
+        if step < nz:
+            first(step)
+        if 0 <= step - 1 < nz:
+            second(step - 1)
+        if 0 <= step - 2 < nz:
+            third(step - 2)
+    for copy in sent:
+        copy.wait_send()
+
+
+def reduce(part, n_pre, n_br):
+    nz = n_pre // 4
+    piece = part.shape[-2:]
+    part = part.reshape((nz, 2, 2, n_br, 2) + piece)
+    copies = nz + nz * (1 + (n_br - 1) + (n_br - 1) + 1) + nz - 1
+    return pl.pallas_call(
+        functools.partial(reduce_kernel, nz, n_br),
+        out_shape=jax.ShapeDtypeStruct((2,) + piece, BF16),
+        in_specs=[pl.BlockSpec(memory_space=pltpu.VMEM)],
+        out_specs=pl.BlockSpec(memory_space=pltpu.VMEM),
+        scratch_shapes=[
+            pltpu.VMEM((nz, 2, n_br, 2) + piece, BF16),
+            pltpu.VMEM((nz, n_br) + piece, BF16),
+            pltpu.VMEM((nz, n_br, 2) + piece, BF16),
+            pltpu.VMEM((nz, n_br) + piece, BF16),
+            pltpu.VMEM((nz,) + piece, BF16),
+            pltpu.VMEM((max(nz - 1, 1), 2) + piece, BF16),
+            pltpu.VMEM((max(nz - 1, 1), 2) + piece, BF16),
+            pltpu.SemaphoreType.DMA((copies,)),
+            pltpu.SemaphoreType.DMA((nz,)),
+            pltpu.SemaphoreType.DMA((nz,)),
+            pltpu.SemaphoreType.DMA((nz, n_br)),
+            pltpu.SemaphoreType.DMA((nz, n_br)),
+            pltpu.SemaphoreType.DMA((nz,)),
+            pltpu.SemaphoreType.DMA((max(nz - 1, 1),)),
+        ],
+        compiler_params=pltpu.CompilerParams(
+            collective_id=1, has_side_effects=True, vmem_limit_bytes=48 * 1024 * 1024
+        ),
+        name="reduce_gradients",
+    )(part)
 
 
 def per_group(x, groups):
@@ -150,8 +379,7 @@
     place = jnp.stack([pre, br, jnp.int32(per_br)])
 
     kv = jnp.stack([prompt_key_rows, prompt_value_rows])
-    kv_all = lax.all_gather(kv, ("pre", "br"), axis=0, tiled=False)
-    kv_all = kv_all.reshape(n_pre, n_br, 2, prow, cols)
+    kv_all = gather(kv, n_pre, n_br)
 
     usable = (resp_segment >= 0)[:, None]
     rnorm = per_group(jnp.where(usable, resp_lse * LOG2E, 1e30), groups)
@@ -205,7 +433,7 @@
             ],
         ),
         out_shape=[
-            jax.ShapeDtypeStruct((n_pre, n_br, 2, prow, cols), F32),
+            jax.ShapeDtypeStruct((n_pre, n_br, 2, prow, cols), BF16),
             jax.ShapeDtypeStruct(resp_query.shape, BF16),
             jax.ShapeDtypeStruct(response_key_rows.shape, BF16),
             jax.ShapeDtypeStruct(response_value_rows.shape, BF16),
@@ -228,10 +456,8 @@
         pnorm,
         pdelta,
     )
-    total = lax.psum_scatter(
-        dkv.reshape(n_pre * n_br, 2, prow, cols), ("pre", "br"), scatter_dimension=0, tiled=False
-    )
-    return pdq, total[0].astype(BF16), total[1].astype(BF16), rdq, rdk, rdv
+    total = reduce(dkv, n_pre, n_br)
+    return pdq, total[0], total[1], rdq, rdk, rdv
 
 
 def solution(mesh):

time: 308 us -> 116 us (0.38)
  waiting for transfers between devices: 250 us -> 0 us
  Pallas kernels: 28.5 us -> 97.5 us
  between operations: 14.1 us -> 0.78 us
    reduce_scatter x1 -> x0, waiting for transfers between devices: 188 us -> none  [local(): lax.psum_scatter(dkv.reshape(n_pre * n_br, 2, prow, cols), ('pre', 'br'),...]
    pallas_call x0 -> x2, Pallas kernels: none -> 69.3 us  [the longest x1 36.6 us: reduce(): pl.pallas_call(functools.partial(reduce_kernel, nz, n_br), out_shape=jax....]
    all_gather x1 -> x0, waiting for transfers between devices: 62.2 us -> none  [local(): kv_all = lax.all_gather(kv, ('pre', 'br'), axis=0, tiled=False)]
    unnamed x12 -> x22, local copies, waits for them, and re-layouts: 6.34 us -> 4.97 us
  transfers between devices with their start and end apart: 2 -> 0, of which waited for: 2 -> 0; matrix products, arithmetic and copies ran while one was open for 2% -> 0% of each run, Pallas kernels for 0% -> 0%
where the time goes in v2:
time: 116 us; the launch traced here: 115 us
  Pallas kernels  97.5 us (84%)
  local copies, waits for them, and re-layouts  11.2 us (10%)
  other arithmetic  5.46 us (5%)
    pallas_call x1, Pallas kernels, reduce(): pl.pallas_call(functools.partial(reduce_kernel, nz, n_br), out_shape=jax....  36.6 us
    pallas_call x1, Pallas kernels, gather(): pl.pallas_call(functools.partial(gather_kernel, nz, n_br), out_shape=jax....  32.7 us
    pallas_call x1, Pallas kernels, local(): pl.pallas_call(functools.partial(attention_kernel, chunk_blocks), grid_sp...  28.2 us
    unnamed x22, local copies, waits for them, and re-layouts  4.97 us
    reshape x4, local copies, waits for them, and re-layouts, per_group(): return x.T.reshape(groups, 1, heads // groups * rows)  2.87 us

profile of v2, /device:TPU:0, one launch (start us, length us, event | category | flops | bytes accessed | tf_op | source)
XLA Modules:
  0.0 114.9 jit_solution(6408868786321597750)
XLA Ops:
  0.6 0.0 copy-start.2
  0.6 0.0 copy-start.6
  0.7 0.0 copy-start.5
  0.7 0.0 copy-start.1
  0.7 0.0 copy-start.4
  0.7 0.0 copy-start.3
  0.7 0.6 pad_add_fusion.place
  1.3 1.0 broadcast_compare_fusion
  2.3 1.4 %reshape.74.pdelta_ref = f32[4,1,512]{2,1,0:T(1,128)} reshape(f32[32,64]{1,0:T(8,128)} %bitcast.19) | data formatting | bytes 16384 | tf_op jit(solution)/shard_map/reshape | solution.py:351
  3.7 0.7 multiply_bitcast_fusion
  4.4 0.7 reshape.73.pnorm_ref
  5.1 0.8 select_bitcast_fusion
  5.9 0.1 copy.19
  6.0 0.1 reshape.71.rnorm_ref
  6.1 0.8 copy.20
  6.9 0.7 reshape.72.rdelta_ref
  7.6 0.8 fusion.1
  8.4 1.5 %pad_maximum_fusion.own_ref = bf16[2,64,512]{2,1,0:T(8,128)(2,1)} fusion(bf16[1,64,512]{2,1,0:T(8,128)(2,1)} %bitcast.16, bf16[1,64,512]{2,1,0:T(8,128)(2,1)} %bitcast.17), kind=kLoop, calls=%fused_computation | loop fusion | flops 65536 | bytes 262144 | tf_op jit(solution)/shard_map/stack | solution.py:381
  10.0 0.7 tile.4
  10.7 1.1 tile.10.bias_ref
  11.7 32.7 %gather_keys.1.kv_ref = bf16[16,2,2,64,512]{4,3,2,1,0:T(8,128)(2,1)} custom-call(bf16[2,64,512]{2,1,0:T(8,128)(2,1)} %pad_maximum_fusion.own_ref), custom_call_target="tpu_custom_call" | custom-call | tf_op jit(solution)/shard_map/gather_keys/pallas_call | solution.py:219
  44.4 0.0 copy-done.2
  44.5 0.0 copy-done.6
  44.5 0.0 copy-done.5
  44.5 0.0 copy-done.1
  44.5 0.0 copy-done.4
  44.5 0.0 copy-done.3
  44.5 0.0 copy-start.7
  44.5 0.7 copy-done.7
  45.2 0.0 copy-start.8
  45.2 0.7 copy-done.8
  45.9 0.0 copy-start.9
  45.9 0.7 copy-done.9
  46.6 0.0 copy-start.10
  46.6 0.7 copy-done.10
  47.3 28.2 %attention.1 = (bf16[16,2,2,64,512]{4,3,2,1,0:T(8,128)(2,1)}, bf16[64,8192]{1,0:T(8,128)(2,1)}, bf16[64,1024]{1,0:T(8,128)(2,1)}, bf16[64,1024]{1,0:T(8,128)(2,1)}, bf16[64,4096]{1,0:T(8,128)(2,1)}) custom-call(s32[3]{0:T(128)S(1)} %copy-done.10, bf16[16,2,2,64,512]{4,3,2,1,0:T(8,128)(2,1)} %gather_keys.1.kv_ref, bf16[64,8192]{1,0:T(8,128)(2,1)S(1)} %copy-done.1, ...), custom_call_target="tpu_custom_call" | custom-call | tf_op jit(solution)/shard_map/attention/pallas_call | solution.py:404
  75.5 0.0 copy-start
  75.5 2.2 %copy-done = bf16[16,2,2,64,512]{4,3,2,1,0:T(8,128)(2,1)S(1)} copy-done((bf16[16,2,2,64,512]{4,3,2,1,0:T(8,128)(2,1)S(1)}, bf16[16,2,2,64,512]{4,3,2,1,0:T(8,128)(2,1)}, u32[]{:S(2)}) %copy-start) | copy-done | bytes 4194328
  77.7 36.6 %reduce_gradients.1 = bf16[2,64,512]{2,1,0:T(8,128)(2,1)S(1)} custom-call(bf16[4,2,2,2,2,64,512]{6,5,4,3,2,1,0:T(8,128)(2,1)S(1)} %bitcast.15), custom_call_target="tpu_custom_call" | custom-call | tf_op jit(solution)/shard_map/reduce_gradients/pallas_call | solution.py:321
  114.3 0.7 slice_bitcast_fusion
Async XLA Ops:
  0.6 43.8 %copy-start.2 = (bf16[64,8192]{1,0:T(8,128)(2,1)S(1)}, bf16[64,8192]{1,0:T(8,128)(2,1)}, u32[]{:S(2)}) copy-start(bf16[64,8192]{1,0:T(8,128)(2,1)} %rgo_ref.1) | copy-start | bytes 3145732
  0.6 43.8 %copy-start.6 = (bf16[64,1024]{1,0:T(8,128)(2,1)S(1)}, bf16[64,1024]{1,0:T(8,128)(2,1)}, u32[]{:S(2)}) copy-start(bf16[64,1024]{1,0:T(8,128)(2,1)} %rv_ref.1) | copy-start | bytes 393220
  0.7 43.8 %copy-start.5 = (bf16[64,1024]{1,0:T(8,128)(2,1)S(1)}, bf16[64,1024]{1,0:T(8,128)(2,1)}, u32[]{:S(2)}) copy-start(bf16[64,1024]{1,0:T(8,128)(2,1)} %rk_ref.1) | copy-start | bytes 393220
  0.7 43.8 %copy-start.1 = (bf16[64,8192]{1,0:T(8,128)(2,1)S(1)}, bf16[64,8192]{1,0:T(8,128)(2,1)}, u32[]{:S(2)}) copy-start(bf16[64,8192]{1,0:T(8,128)(2,1)} %rq_ref.1) | copy-start | bytes 3145732
  0.7 43.8 %copy-start.4 = (bf16[64,4096]{1,0:T(8,128)(2,1)S(1)}, bf16[64,4096]{1,0:T(8,128)(2,1)}, u32[]{:S(2)}) copy-start(bf16[64,4096]{1,0:T(8,128)(2,1)} %pgo_ref.1) | copy-start | bytes 1572868
  0.7 43.8 %copy-start.3 = (bf16[64,4096]{1,0:T(8,128)(2,1)S(1)}, bf16[64,4096]{1,0:T(8,128)(2,1)}, u32[]{:S(2)}) copy-start(bf16[64,4096]{1,0:T(8,128)(2,1)} %pq_ref.1) | copy-start | bytes 1572868
  44.5 0.7 copy-start.7
  45.2 0.7 copy-start.8
  45.9 0.7 copy-start.9
  46.6 0.7 copy-start.10
  75.5 2.2 %copy-start = (bf16[16,2,2,64,512]{4,3,2,1,0:T(8,128)(2,1)S(1)}, bf16[16,2,2,64,512]{4,3,2,1,0:T(8,128)(2,1)}, u32[]{:S(2)}) copy-start(bf16[16,2,2,64,512]{4,3,2,1,0:T(8,128)(2,1)} %get-tuple-element.12) | copy-start | bytes 12582916

commit v3 on v1

v3 whole, which is shorter than its diff:
```python
import functools

import jax
import jax.numpy as jnp
from jax import lax
from jax.experimental import pallas as pl
from jax.experimental.pallas import tpu as pltpu
from jax.sharding import PartitionSpec as P

HEAD = 128
SCALE = HEAD ** (-0.5)
LOG2E = 1.4426950408889634
F32 = jnp.float32
BF16 = jnp.bfloat16


def dot(a, b, ca, cb):
    return lax.dot_general(a, b, (((ca,), (cb,)), ((), ())), preferred_element_type=F32)


def stack_heads(block):
    ratio = block.shape[1] // HEAD
    return jnp.concatenate([block[:, h * HEAD : (h + 1) * HEAD] for h in range(ratio)], 0)


def spread_heads(dq_t, rows):
    dq = dq_t.T
    ratio = dq.shape[0] // rows
    return jnp.concatenate([dq[h * rows : (h + 1) * rows] for h in range(ratio)], 1)


def terms(k, v, q, go, norm, delta, bias):
    s = dot(k, q, 1, 1)
    z = s * (SCALE * LOG2E) - norm
    if bias is not None:
        z = z + bias
    w = jnp.exp2(z)
    ds = w * (dot(v, go, 1, 1) - delta)
    wb = w.astype(BF16)
    dsb = ds.astype(BF16)
    return dot(dsb, q, 1, 0) * SCALE, dot(wb, go, 1, 0), dot(k, dsb, 0, 0)


def position(nz, ny):
    pre = lax.axis_index("pre")
    y = lax.axis_index("br")
    z = pre // 4
    x = lax.rem(pre // 2, 2)
    c = lax.rem(pre, 2)
    index = lambda zz, xx, cc: (zz * 2 + xx) * 2 + cc
    around_z = [lax.rem(z + d, nz) for d in range(1, nz)]
    around_y = [lax.rem(y + d, ny) for d in range(1, ny)]
    return z, x, c, y, index, around_z, around_y


def greet(targets):
    barrier = pltpu.get_barrier_semaphore()
    for target in targets:
        pl.semaphore_signal(barrier, inc=1, device_id=target, device_id_type=pl.DeviceIdType.MESH)
    pl.semaphore_wait(barrier, len(targets))


def fused_kernel(
    nz,
    ny,
    own_ref,
    rq_ref,
    rgo_ref,
    rnorm_ref,
    rdelta_ref,
    bias_ref,
    rk_ref,
    rv_ref,
    pq_ref,
    pgo_ref,
    pnorm_ref,
    pdelta_ref,
    out_ref,
    rdq_ref,
    rdk_ref,
    rdv_ref,
    pdq_ref,
    kv,
    part,
    racc,
    pacc,
    r0,
    rx,
    ry,
    ryk,
    rxv,
    sz,
    rz,
    fin,
    send_sem,
    recv_sem,
    local_sem,
    q0,
    qx,
    qy,
    qyk,
    qxv,
    qz,
):
    z, x, c, y, index, around_z, around_y = position(nz, ny)
    sibling = (index(z, x, 1 - c), y)
    x_side = (index(z, 1 - x, c), y)
    y_side = [(index(z, x, c), yy) for yy in around_y]
    z_side = [(index(zz, x, c), y) for zz in around_z]
    greet([sibling, x_side] + y_side + z_side)
    order = [z] + around_z
    sent = []
    rows = rk_ref.shape[0]
    groups = rk_ref.shape[1] // HEAD
    _, prow, cols = own_ref.shape
    per_br = cols // HEAD
    wide = rq_ref.shape[1] // groups
    chunk = 4 * prow

    def push(src, dst, sem, target):
        copy = pltpu.make_async_remote_copy(
            src_ref=src,
            dst_ref=dst,
            send_sem=send_sem.at[len(sent)],
            recv_sem=sem,
            device_id=target,
            device_id_type=pl.DeviceIdType.MESH,
        )
        copy.start()
        sent.append(copy)

    def landed(at, sem):
        pltpu.make_async_copy(at, at, sem).wait()

    def send(zz, xx, yy, t, target, mine=False):
        slot = index(zz, xx, c)
        src = own_ref.at[t] if mine else kv.at[slot, yy, t]
        push(src, kv.at[slot, yy, t], recv_sem.at[slot, yy, t], target)

    def arrive(zz, xx, yy, cc, t):
        slot = index(zz, xx, cc)
        landed(kv.at[slot, yy, t], recv_sem.at[slot, yy, t])

    def column(i):
        zz = order[i]
        for t in range(2):
            if i > 0:
                arrive(zz, x, y, c, t)
            send(zz, x, y, t, x_side, i == 0)
            for target in y_side:
                send(zz, x, y, t, target, i == 0)
            send(zz, x, y, t, sibling, i == 0)

    def second(i):
        zz = order[i]
        for t in range(2):
            arrive(zz, 1 - x, y, c, t)
            if t == 0:
                for target in y_side:
                    send(zz, 1 - x, y, 0, target)
            send(zz, 1 - x, y, t, sibling)
            for yy in around_y:
                arrive(zz, x, yy, c, t)
                if t == 1:
                    send(zz, x, yy, 1, x_side)
                send(zz, x, yy, t, sibling)

    def third(i):
        zz = order[i]
        for t in range(2):
            for yy in around_y:
                arrive(zz, 1 - x, yy, c, t)
                send(zz, 1 - x, yy, t, sibling)

    def from_sibling(i):
        for xx in range(2):
            for yy in [y] + around_y:
                for t in range(2):
                    arrive(order[i], xx, yy, 1 - c, t)

    def cut(ref, g, width):
        return ref[:, pl.ds(pl.multiple_of(g * width, width), width)]

    def near(g, carry):
        at = pl.ds(pl.multiple_of(g * HEAD, HEAD), HEAD)
        rq = stack_heads(cut(rq_ref, g, wide))
        rgo = stack_heads(cut(rgo_ref, g, wide))
        dk, dv, dq = terms(
            rk_ref[:, at], rv_ref[:, at], rq, rgo, rnorm_ref[g], rdelta_ref[g], bias_ref[...]
        )
        rdk_ref[:, at] = dk.astype(BF16)
        rdv_ref[:, at] = dv.astype(BF16)
        racc[g] = dq
        return carry

    def far(i, g, carry):
        zz = order[i]
        owner = g // per_br
        lane = pl.ds(pl.multiple_of(lax.rem(g, per_br) * HEAD, HEAD), HEAD)
        k = kv[pl.ds(zz * 4, 4), owner, 0, :, lane].reshape(chunk, HEAD)
        v = kv[pl.ds(zz * 4, 4), owner, 1, :, lane].reshape(chunk, HEAD)
        rq = stack_heads(cut(rq_ref, g, wide))
        rgo = stack_heads(cut(rgo_ref, g, wide))
        dk, dv, dq = terms(k, v, rq, rgo, rnorm_ref[g], rdelta_ref[g], None)
        racc[g] += dq

        def put(dk, dv):
            for xx in range(2):
                for cc in range(2):
                    first_row = (xx * 2 + cc) * prow
                    piece = slice(first_row, first_row + prow)
                    part[zz, xx, cc, owner, 0, :, lane] = dk[piece].astype(BF16)
                    part[zz, xx, cc, owner, 1, :, lane] = dv[piece].astype(BF16)

        with_prompt = (owner == y) & (zz <= z)

        @pl.when(with_prompt)
        def _():
            own = g - y * per_br
            pq = stack_heads(cut(pq_ref, own, wide))
            pgo = stack_heads(cut(pgo_ref, own, wide))
            bias = None
            if i == 0:
                key = lax.broadcasted_iota(jnp.int32, (chunk, pq.shape[0]), 0)
                row = lax.rem(lax.broadcasted_iota(jnp.int32, (chunk, pq.shape[0]), 1), prow)
                bias = jnp.where(key <= row + (x * 2 + c) * prow, 0.0, -1e30)
            pdk, pdv, pdq = terms(k, v, pq, pgo, pnorm_ref[own], pdelta_ref[own], bias)
            if i == 0:
                pacc[own] = pdq
            else:
                pacc[own] += pdq
            put(dk + pdk, dv + pdv)

        @pl.when(jnp.logical_not(with_prompt))
        def _():
            put(dk, dv)

        return carry

    def compute(i, half):
        low, high = (0, groups // 2) if half == 0 else (groups // 2, groups)
        lax.fori_loop(low, high, functools.partial(far, i), 0)

    def swap(i):
        push(part.at[order[i], :, 1 - c], r0.at[i], q0.at[i], sibling)

    def reduce_first(i):
        landed(r0.at[i], q0.at[i])
        for xx in range(2):
            for yy in range(ny):
                own = part[order[i], xx, c, yy].astype(F32)
                r0[i, xx, yy] = (own + r0[i, xx, yy].astype(F32)).astype(BF16)
        push(r0.at[i, 1 - x, :, 0], rx.at[i], qx.at[i], x_side)
        for target, yy in zip(y_side, around_y):
            push(r0.at[i, :, yy, 1], ry.at[i, y], qy.at[i, y], target)

    def reduce_second(i):
        landed(rx.at[i], qx.at[i])
        rx[i] = (r0[i, x, :, 0].astype(F32) + rx[i].astype(F32)).astype(BF16)
        for target, yy in zip(y_side, around_y):
            push(rx.at[i, yy], ryk.at[i, y], qyk.at[i, y], target)
        total = r0[i, :, y, 1].astype(F32)
        for yy in around_y:
            landed(ry.at[i, yy], qy.at[i, yy])
            total = total + ry[i, yy].astype(F32)
        ry[i, y] = total.astype(BF16)
        push(ry.at[i, y, 1 - x], rxv.at[i], qxv.at[i], x_side)

    def reduce_third(i):
        total_k = rx[i, y].astype(F32)
        for yy in around_y:
            landed(ryk.at[i, yy], qyk.at[i, yy])
            total_k = total_k + ryk[i, yy].astype(F32)
        landed(rxv.at[i], qxv.at[i])
        total_v = ry[i, y, x].astype(F32) + rxv[i].astype(F32)
        if i == 0:
            fin[0] = total_k
            fin[1] = total_v
        else:
            sz[i - 1, 0] = total_k.astype(BF16)
            sz[i - 1, 1] = total_v.astype(BF16)
            push(sz.at[i - 1], rz.at[i - 1], qz.at[i - 1], z_side[i - 1])

    for target in z_side:
        for t in range(2):
            send(z, x, y, t, target, True)
    keep = pltpu.make_async_copy(own_ref, kv.at[index(z, x, c), y], local_sem)
    keep.start()
    column(0)
    lax.fori_loop(0, groups, near, 0)
    second(0)
    if nz > 1:
        column(1)
    third(0)
    keep.wait()
    for i in range(nz):
        from_sibling(i)
        compute(i, 0)
        if i + 1 < nz:
            second(i + 1)
        if i + 2 < nz:
            column(i + 2)
        if i >= 1:
            reduce_first(i - 1)
        compute(i, 1)
        swap(i)
        if i + 1 < nz:
            third(i + 1)
        if i >= 1:
            reduce_second(i - 1)
        if i >= 2:
            reduce_third(i - 2)

    def finish(g, carry):
        at = pl.ds(pl.multiple_of(g * wide, wide), wide)
        rdq_ref[:, at] = (spread_heads(racc[g], rows) * SCALE).astype(BF16)
        return carry

    def finish_prompt(g, carry):
        at = pl.ds(pl.multiple_of(g * wide, wide), wide)
        pdq_ref[:, at] = (spread_heads(pacc[g], prow) * SCALE).astype(BF16)
        return carry

    lax.fori_loop(0, per_br, finish_prompt, 0)
    reduce_first(nz - 1)
    if nz > 1:
        reduce_third(nz - 2)
    lax.fori_loop(0, groups, finish, 0)
    reduce_second(nz - 1)
    reduce_third(nz - 1)
    total = fin[...]
    for j in range(nz - 1):
        landed(rz.at[j], qz.at[j])
        total = total + rz[j].astype(F32)
    out_ref[...] = total.astype(BF16)
    for copy in sent:
        copy.wait_send()


def per_group(x, groups):
    rows, heads = x.shape
    return x.T.reshape(groups, 1, heads // groups * rows)


def local(
    n_pre,
    n_br,
    prompt_query,
    prompt_key_rows,
    prompt_value_rows,
    prompt_grad_out,
    prompt_lse,
    prompt_delta,
    resp_query,
    response_key_rows,
    response_value_rows,
    resp_grad_out,
    resp_lse,
    resp_delta,
    resp_segment,
):
    prow, cols = prompt_key_rows.shape
    rows, width = response_key_rows.shape
    groups = width // HEAD
    per_br = cols // HEAD
    ratio = resp_query.shape[1] // width
    kv = jnp.stack([prompt_key_rows, prompt_value_rows])
    usable = (resp_segment >= 0)[:, None]
    rnorm = per_group(jnp.where(usable, resp_lse * LOG2E, 1e30), groups)
    rdelta = per_group(resp_delta, groups)
    pnorm = per_group(prompt_lse * LOG2E, per_br)
    pdelta = per_group(prompt_delta, per_br)
    index = jnp.arange(rows, dtype=jnp.int32)
    seen = (resp_segment[:, None] == resp_segment[None, :]) & (index[:, None] <= index[None, :])
    bias = jnp.tile(jnp.where(seen, 0.0, -1e30), (1, ratio))

    nz = n_pre // 4
    piece = (prow, cols)
    copies = 2 * (nz - 1) + nz * (2 * (1 + n_br) + (n_br - 1) * 2 + 2 * n_br + 2 * (n_br - 1))
    copies += nz + nz * (1 + (n_br - 1) + (n_br - 1) + 1) + nz - 1
    others = max(nz - 1, 1)
    sem = pltpu.SemaphoreType.DMA
    vmem = pl.BlockSpec(memory_space=pltpu.VMEM)
    total, rdq, rdk, rdv, pdq = pl.pallas_call(
        functools.partial(fused_kernel, nz, n_br),
        in_specs=[vmem] * 12,
        out_specs=[vmem] * 5,
        out_shape=[
            jax.ShapeDtypeStruct((2,) + piece, BF16),
            jax.ShapeDtypeStruct(resp_query.shape, BF16),
            jax.ShapeDtypeStruct(response_key_rows.shape, BF16),
            jax.ShapeDtypeStruct(response_value_rows.shape, BF16),
            jax.ShapeDtypeStruct(prompt_query.shape, BF16),
        ],
        scratch_shapes=[
            pltpu.VMEM((n_pre, n_br, 2) + piece, BF16),
            pltpu.VMEM((nz, 2, 2, n_br, 2) + piece, BF16),
            pltpu.VMEM((groups, HEAD, ratio * rows), F32),
            pltpu.VMEM((per_br, HEAD, ratio * prow), F32),
            pltpu.VMEM((nz, 2, n_br, 2) + piece, BF16),
            pltpu.VMEM((nz, n_br) + piece, BF16),
            pltpu.VMEM((nz, n_br, 2) + piece, BF16),
            pltpu.VMEM((nz, n_br) + piece, BF16),
            pltpu.VMEM((nz,) + piece, BF16),
            pltpu.VMEM((others, 2) + piece, BF16),
            pltpu.VMEM((others, 2) + piece, BF16),
            pltpu.VMEM((2,) + piece, F32),
            sem((copies,)),
            sem((n_pre, n_br, 2)),
            sem,
            sem((nz,)),
            sem((nz,)),
            sem((nz, n_br)),
            sem((nz, n_br)),
            sem((nz,)),
            sem((others,)),
        ],
        compiler_params=pltpu.CompilerParams(
            collective_id=0, has_side_effects=True, vmem_limit_bytes=52 * 1024 * 1024
        ),
        name="attention_backward",
    )(
        kv,
        resp_query,
        resp_grad_out,
        rnorm,
        rdelta,
        bias,
        response_key_rows,
        response_value_rows,
        prompt_query,
        prompt_grad_out,
        pnorm,
        pdelta,
    )
    return pdq, total[0], total[1], rdq, rdk, rdv


def solution(mesh):
    both = P("pre", "br")
    own = P(("pre", "br"), None)
    in_specs = (both,) * 6 + (own,) * 6 + (P(("pre", "br")),)
    out_specs = (both,) * 3 + (own,) * 3
    body = functools.partial(local, mesh.shape["pre"], mesh.shape["br"])
    return jax.shard_map(body, mesh=mesh, in_specs=in_specs, out_specs=out_specs, check_vma=False)
```

time: 308 us -> 84 us (0.27)
  waiting for transfers between devices: 250 us -> 0 us
  Pallas kernels: 28.5 us -> 74.1 us
  between operations: 14.1 us -> 0.75 us
  other arithmetic: 5.6 us -> 0.17 us
    reduce_scatter x1 -> x0, waiting for transfers between devices: 188 us -> none  [local(): lax.psum_scatter(dkv.reshape(n_pre * n_br, 2, prow, cols), ('pre', 'br'),...]
    all_gather x1 -> x0, waiting for transfers between devices: 62.2 us -> none  [local(): kv_all = lax.all_gather(kv, ('pre', 'br'), axis=0, tiled=False)]
    pallas_call x1, Pallas kernels: 28.5 us -> 74.1 us  [local(): pl.pallas_call(functools.partial(fused_kernel, nz, n_br), in_specs=[vmem]...]
    unnamed x12 -> x24, local copies, waits for them, and re-layouts: 6.34 us -> 6.52 us
  transfers between devices with their start and end apart: 2 -> 0, of which waited for: 2 -> 0; matrix products, arithmetic and copies ran while one was open for 2% -> 0% of each run, Pallas kernels for 0% -> 0%
where the time goes in v3:
time: 84 us; the launch traced here: 83.5 us
  Pallas kernels  74.1 us (88%)
  local copies, waits for them, and re-layouts  8.51 us (10%)
    pallas_call x1, Pallas kernels, local(): pl.pallas_call(functools.partial(fused_kernel, nz, n_br), in_specs=[vmem]...  74.1 us
    unnamed x24, local copies, waits for them, and re-layouts  6.52 us

profile of v3, /device:TPU:0, one launch (start us, length us, event | category | flops | bytes accessed | tf_op | source)
XLA Modules:
  0.0 83.5 jit_solution(15604700309467856484)
XLA Ops:
  0.6 0.0 copy-start.9
  0.6 0.0 copy-start.8
  0.7 0.6 copy-done.9
  1.3 0.8 reshape.71.pdelta_ref
  2.1 0.0 copy-done.8
  2.1 0.0 copy-start.6
  2.1 0.1 reshape.70.pnorm_ref
  2.2 0.7 copy-done.6
  2.9 0.1 select_bitcast_fusion
  2.9 0.1 copy.19
  3.0 0.0 copy-start.7
  3.0 0.1 reshape.68.rnorm_ref
  3.1 0.7 copy-done.7
  3.8 0.0 copy-start.4
  3.8 0.0 copy-start.5
  3.8 0.1 copy.20
  3.9 0.0 copy-start
  3.9 0.1 reshape.69.rdelta_ref
  4.0 0.1 fusion.1
  4.0 0.6 copy-done.4
  4.6 0.0 copy-done.5
  4.7 0.0 copy-start.1
  4.7 0.0 copy-start.2
  4.7 0.1 tile.10.bias_ref
  4.8 0.1 copy-done
  4.9 0.7 copy-done.1
  5.6 0.0 copy-done.2
  5.7 74.1 %attention_backward.1 = (bf16[2,64,512]{2,1,0:T(8,128)(2,1)S(1)}, bf16[64,8192]{1,0:T(8,128)(2,1)}, bf16[64,1024]{1,0:T(8,128)(2,1)S(1)}, bf16[64,1024]{1,0:T(8,128)(2,1)S(1)}, bf16[64,4096]{1,0:T(8,128)(2,1)S(1)}) custom-call(bf16[2,64,512]{2,1,0:T(8,128)(2,1)S(1)} %pad_maximum_fusion.own_ref, bf16[64,8192]{1,0:T(8,128)(2,1)} %rq_ref.1, ...), custom_call_target="tpu_custom_call" | custom-call | tf_op jit(solution)/shard_map/attention_backward/pallas_call | solution.py:384
  79.8 0.0 copy-start.3
  79.8 0.7 slice_bitcast_fusion
  80.5 0.8 copy.25
  81.2 0.0 copy-done.3
  81.3 1.0 %copy.26 = bf16[64,8192]{1,0:T(8,128)(2,1)} copy(bf16[64,8192]{1,0:T(8,128)(2,1)S(1)} %copy-done.3) | data formatting | bytes 2097152
  82.2 0.7 copy.27
  82.9 0.7 copy.28
  (4 shorter events, 0.0 us)
Async XLA Ops:
  0.6 0.7 copy-start.9
  0.6 1.5 %copy-start.8 = (f32[64,32]{0,1:T(8,128)S(1)}, f32[64,32]{0,1:T(8,128)}, u32[]{:S(2)}) copy-start(f32[64,32]{0,1:T(8,128)} %param.17) | copy-start | bytes 24580
  2.1 0.8 copy-start.6
  3.0 0.8 copy-start.7
  3.8 0.8 %copy-start.4 = (bf16[64,512]{1,0:T(8,128)(2,1)S(1)}, bf16[64,512]{1,0:T(8,128)(2,1)}, u32[]{:S(2)}) copy-start(bf16[64,512]{1,0:T(8,128)(2,1)} %param.15) | copy-start | bytes 196612
  3.8 0.9 %copy-start.5 = (bf16[64,512]{1,0:T(8,128)(2,1)S(1)}, bf16[64,512]{1,0:T(8,128)(2,1)}, u32[]{:S(2)}) copy-start(bf16[64,512]{1,0:T(8,128)(2,1)} %param.14) | copy-start | bytes 196612
  3.9 1.1 %copy-start = (bf16[64,4096]{1,0:T(8,128)(2,1)S(1)}, bf16[64,4096]{1,0:T(8,128)(2,1)}, u32[]{:S(2)}) copy-start(bf16[64,4096]{1,0:T(8,128)(2,1)} %pq_ref.1) | copy-start | bytes 1572868
  4.7 0.9 %copy-start.1 = (bf16[64,1024]{1,0:T(8,128)(2,1)S(1)}, bf16[64,1024]{1,0:T(8,128)(2,1)}, u32[]{:S(2)}) copy-start(bf16[64,1024]{1,0:T(8,128)(2,1)} %rk_ref.1) | copy-start | bytes 393220
  4.7 1.0 %copy-start.2 = (bf16[64,1024]{1,0:T(8,128)(2,1)S(1)}, bf16[64,1024]{1,0:T(8,128)(2,1)}, u32[]{:S(2)}) copy-start(bf16[64,1024]{1,0:T(8,128)(2,1)} %rv_ref.1) | copy-start | bytes 393220
  79.8 1.5 %copy-start.3 = (bf16[64,8192]{1,0:T(8,128)(2,1)S(1)}, bf16[64,8192]{1,0:T(8,128)(2,1)}, u32[]{:S(2)}) copy-start(bf16[64,8192]{1,0:T(8,128)(2,1)} %get-tuple-element.27) | copy-start | bytes 3145732

commit v4 on v3

--- a/solution.py
+++ b/solution.py
@@ -75,7 +75,8 @@
     pgo_ref,
     pnorm_ref,
     pdelta_ref,
-    out_ref,
+    pdk_ref,
+    pdv_ref,
     rdq_ref,
     rdk_ref,
     rdv_ref,
@@ -241,11 +242,18 @@
         low, high = (0, groups // 2) if half == 0 else (groups // 2, groups)
         lax.fori_loop(low, high, functools.partial(far, i), 0)
 
-    def swap(i):
-        push(part.at[order[i], :, 1 - c], r0.at[i], q0.at[i], sibling)
+    halves = 2 if ny % 2 == 0 else 1
+
+    def owners(half):
+        return pl.ds(half * (ny // halves), ny // halves)
+
+    def swap(i, half):
+        at = owners(half)
+        push(part.at[order[i], :, 1 - c, at], r0.at[i, :, at], q0.at[i, half], sibling)
 
     def reduce_first(i):
-        landed(r0.at[i], q0.at[i])
+        for half in range(halves):
+            landed(r0.at[i, :, owners(half)], q0.at[i, half])
         for xx in range(2):
             for yy in range(ny):
                 own = part[order[i], xx, c, yy].astype(F32)
@@ -296,6 +304,8 @@
     for i in range(nz):
         from_sibling(i)
         compute(i, 0)
+        if halves == 2:
+            swap(i, 0)
         if i + 1 < nz:
             second(i + 1)
         if i + 2 < nz:
@@ -303,7 +313,7 @@
         if i >= 1:
             reduce_first(i - 1)
         compute(i, 1)
-        swap(i)
+        swap(i, halves - 1)
         if i + 1 < nz:
             third(i + 1)
         if i >= 1:
@@ -332,7 +342,8 @@
     for j in range(nz - 1):
         landed(rz.at[j], qz.at[j])
         total = total + rz[j].astype(F32)
-    out_ref[...] = total.astype(BF16)
+    pdk_ref[...] = total[0].astype(BF16)
+    pdv_ref[...] = total[1].astype(BF16)
     for copy in sent:
         copy.wait_send()
 
@@ -377,16 +388,17 @@
     nz = n_pre // 4
     piece = (prow, cols)
     copies = 2 * (nz - 1) + nz * (2 * (1 + n_br) + (n_br - 1) * 2 + 2 * n_br + 2 * (n_br - 1))
-    copies += nz + nz * (1 + (n_br - 1) + (n_br - 1) + 1) + nz - 1
+    copies += 2 * nz + nz * (1 + (n_br - 1) + (n_br - 1) + 1) + nz - 1
     others = max(nz - 1, 1)
     sem = pltpu.SemaphoreType.DMA
     vmem = pl.BlockSpec(memory_space=pltpu.VMEM)
-    total, rdq, rdk, rdv, pdq = pl.pallas_call(
+    pdk, pdv, rdq, rdk, rdv, pdq = pl.pallas_call(
         functools.partial(fused_kernel, nz, n_br),
         in_specs=[vmem] * 12,
-        out_specs=[vmem] * 5,
+        out_specs=[vmem] * 6,
         out_shape=[
-            jax.ShapeDtypeStruct((2,) + piece, BF16),
+            jax.ShapeDtypeStruct(piece, BF16),
+            jax.ShapeDtypeStruct(piece, BF16),
             jax.ShapeDtypeStruct(resp_query.shape, BF16),
             jax.ShapeDtypeStruct(response_key_rows.shape, BF16),
             jax.ShapeDtypeStruct(response_value_rows.shape, BF16),
@@ -408,7 +420,7 @@
             sem((copies,)),
             sem((n_pre, n_br, 2)),
             sem,
-            sem((nz,)),
+            sem((nz, 2)),
             sem((nz,)),
             sem((nz, n_br)),
             sem((nz, n_br)),
@@ -433,7 +445,7 @@
         pnorm,
         pdelta,
     )
-    return pdq, total[0], total[1], rdq, rdk, rdv
+    return pdq, pdk, pdv, rdq, rdk, rdv
 
 
 def solution(mesh):

time: 84 us -> 84.4 us (level)
    unnamed x24 -> x26, local copies, waits for them, and re-layouts: 6.52 us -> 7.78 us
where the time goes in v4:
time: 84.4 us; the launch traced here: 84 us
  Pallas kernels  74 us (88%)
  local copies, waits for them, and re-layouts  9.11 us (11%)
    pallas_call x1, Pallas kernels, local(): pl.pallas_call(functools.partial(fused_kernel, nz, n_br), in_specs=[vmem]...  74 us
    unnamed x26, local copies, waits for them, and re-layouts  7.78 us

profile of v4, /device:TPU:0, one launch (start us, length us, event | category | flops | bytes accessed | tf_op | source)
XLA Modules:
  0.0 84.0 jit_solution(14875208718450129100)
XLA Ops:
  0.6 0.0 copy-start.9
  0.6 0.0 copy-start.8
  0.7 0.6 copy-done.9
  1.3 0.8 reshape.71.pdelta_ref
  2.1 0.0 copy-done.8
  2.1 0.0 copy-start.6
  2.1 0.1 reshape.70.pnorm_ref
  2.2 0.7 copy-done.6
  2.9 0.1 select_bitcast_fusion
  2.9 0.1 copy.19
  3.0 0.0 copy-start.7
  3.0 0.1 reshape.68.rnorm_ref
  3.1 0.7 copy-done.7
  3.8 0.0 copy-start.4
  3.8 0.0 copy-start.5
  3.8 0.1 copy.20
  3.9 0.0 copy-start
  3.9 0.1 reshape.69.rdelta_ref
  4.0 0.1 fusion.1
  4.0 0.6 copy-done.4
  4.6 0.0 copy-done.5
  4.7 0.0 copy-start.1
  4.7 0.0 copy-start.2
  4.7 0.1 tile.10.bias_ref
  4.8 0.1 copy-done
  4.9 0.7 copy-done.1
  5.6 0.0 copy-done.2
  5.7 74.0 %attention_backward.1 = (bf16[64,512]{1,0:T(8,128)(2,1)S(1)}, bf16[64,512]{1,0:T(8,128)(2,1)S(1)}, bf16[64,8192]{1,0:T(8,128)(2,1)}, bf16[64,1024]{1,0:T(8,128)(...) custom-call(bf16[2,64,512]{2,1,0:T(8,128)(2,1)S(1)} %pad_maximum_fusion.own_ref, ...), custom_call_target="tpu_custom_call" | custom-call | tf_op jit(solution)/shard_map/attention_backward/pallas_call | solution.py:395
  79.7 0.0 copy-start.3
  79.7 0.8 copy.27
  80.5 0.6 copy.28
  81.1 0.6 copy.29
  81.7 0.0 copy-done.3
  81.7 1.0 %copy.30 = bf16[64,8192]{1,0:T(8,128)(2,1)} copy(bf16[64,8192]{1,0:T(8,128)(2,1)S(1)} %copy-done.3) | data formatting | bytes 2097152
  82.7 0.7 copy.31
  83.4 0.7 copy.32
  (4 shorter events, 0.0 us)
Async XLA Ops:
  0.6 0.7 copy-start.9
  0.6 1.5 %copy-start.8 = (f32[64,32]{0,1:T(8,128)S(1)}, f32[64,32]{0,1:T(8,128)}, u32[]{:S(2)}) copy-start(f32[64,32]{0,1:T(8,128)} %param.17) | copy-start | bytes 24580
  2.1 0.8 copy-start.6
  3.0 0.8 copy-start.7
  3.8 0.8 copy-start.4
  3.8 0.9 %copy-start.5 = (bf16[64,512]{1,0:T(8,128)(2,1)S(1)}, bf16[64,512]{1,0:T(8,128)(2,1)}, u32[]{:S(2)}) copy-start(bf16[64,512]{1,0:T(8,128)(2,1)} %param.14) | copy-start | bytes 196612
  3.9 1.1 %copy-start = (bf16[64,4096]{1,0:T(8,128)(2,1)S(1)}, bf16[64,4096]{1,0:T(8,128)(2,1)}, u32[]{:S(2)}) copy-start(bf16[64,4096]{1,0:T(8,128)(2,1)} %pq_ref.1) | copy-start | bytes 1572868
  4.7 0.9 %copy-start.1 = (bf16[64,1024]{1,0:T(8,128)(2,1)S(1)}, bf16[64,1024]{1,0:T(8,128)(2,1)}, u32[]{:S(2)}) copy-start(bf16[64,1024]{1,0:T(8,128)(2,1)} %rk_ref.1) | copy-start | bytes 393220
  4.7 1.0 %copy-start.2 = (bf16[64,1024]{1,0:T(8,128)(2,1)S(1)}, bf16[64,1024]{1,0:T(8,128)(2,1)}, u32[]{:S(2)}) copy-start(bf16[64,1024]{1,0:T(8,128)(2,1)} %rv_ref.1) | copy-start | bytes 393220
  79.7 2.1 %copy-start.3 = (bf16[64,8192]{1,0:T(8,128)(2,1)S(1)}, bf16[64,8192]{1,0:T(8,128)(2,1)}, u32[]{:S(2)}) copy-start(bf16[64,8192]{1,0:T(8,128)(2,1)} %get-tuple-element.27) | copy-start | bytes 3145732
